TPU v7x, 256 devices: a whole 4x4x8 slice. The times are simulated.
256 devices in a mesh: grp: 4 (over x), dom: 64 (over z, y, core).
Axes of the slice: x: 4, y: 4, z: 8, core: 2. Of those that a mesh axis runs over, the one named last changes fastest.
Arguments:
- fine_nodes: bfloat16 [131072, 128], P(('grp', 'dom')), may hold values from -6 to 6
- cotangent: float32 [131072, 128], P(('grp', 'dom')), may hold values from -6 to 6
- msg_weights: bfloat16 [3, 256, 128], replicated, may hold values from -0.375 to 0.375
- msg_biases: float32 [3, 128], replicated, may hold values from -3 to 3
- node_weights: bfloat16 [3, 256, 128], replicated, may hold values from -0.375 to 0.375
- node_biases: float32 [3, 128], replicated, may hold values from -3 to 3
- node_count: int32 [256], P(('grp', 'dom')), may hold values from 256 to 512, as said below
- fine_edges: int32 [256, 2, 3072], P(('grp', 'dom')), may hold values from 0 to 639, as said below
- fine_send: int32 [256, 2, 64], P(('grp', 'dom')), may hold values from 0 to 255, as said below
- pool_map: int32 [256, 512], P(('grp', 'dom')), may hold values from 0 to 127, as said below
- coarse_edges: int32 [256, 2, 384], P(('grp', 'dom')), may hold values from 0 to 79, as said below
- top_map: int32 [256, 64], P(('grp', 'dom')), may hold values from 0 to 2047, as said below
- top_edges: int32 [2, 12288], replicated, may hold values from 0 to 2047
Outputs:
- fine_out: bfloat16 [131072, 128], P(('grp', 'dom'))
- node_grad: float32 [131072, 128], P(('grp', 'dom'))
- msg_weight_grad: float32 [3, 256, 128], replicated
- msg_bias_grad: float32 [3, 128], replicated
- node_weight_grad: float32 [3, 256, 128], replicated
- node_bias_grad: float32 [3, 128], replicated
Inputs may be any that keep to these rules, and one draw needn't show every extreme that they name: `node_count`: some partition has all 512 rows live in every draw. fine_edges[p, 0, e] indexes partition p's fine_ext: a live row of its own, or 512 + r for received row r; fine_edges[p, 1, e] is a live row of partition p. `fine_send`: every listed row is live. `pool_map`: the last partition maps only to its own coarse nodes, below 64. coarse_edges[p, 0, e] indexes partition p's coarse_ext; coarse_edges[p, 1, e] is below 64. `top_map`: the coarse nodes of partition p map only to coarsest nodes (p - 1) * (8) to (p + 2) * 8 - 1, taken modulo 2048; in every partition both ends of that window are used.
All inputs are finite; a program needn't handle non-finite values.
Results may differ from a plain program's by a relative error of at most 0.012.
The roundings to bfloat16 on the way count: a program that leaves them out, or rounds other values in their place, can miss the bound.
Values may be sent and summed in bfloat16 or wider, within the bound.
A program may use at most 128 MiB of HBM per device.

v0:
```python
import functools

import jax
import jax.numpy as jnp
from jax import lax
from jax.experimental import pallas as pl
from jax.experimental.pallas import tpu as pltpu
from jax.sharding import PartitionSpec as P

BF, F32, I32 = jnp.bfloat16, jnp.float32, jnp.int32
MESH = pl.DeviceIdType.MESH
W = 128
TILE = 128
CAP = 128
DOM_SPLIT = (8, 4, 2)
ROWS = 8


def mm(a, b):
    return jnp.dot(a, b, preferred_element_type=F32)


def nt(a, b):
    return lax.dot_general(a, b, (((1,), (1,)), ((), ())), preferred_element_type=F32)


def tn(a, b):
    return lax.dot_general(a, b, (((0,), (0,)), ((), ())), preferred_element_type=F32)


def wide(v):
    high = v.astype(BF)
    return jnp.concatenate([high, (v - high.astype(F32)).astype(BF)], axis=1)


def fold(v):
    return v[:, :W] + v[:, W:]


def nt_split(v, weight):
    high = v.astype(BF)
    return nt(high, weight) + nt((v - high.astype(F32)).astype(BF), weight)


def iota(shape, dim):
    return lax.broadcasted_iota(I32, shape, dim)


def hot(mask):
    return jnp.where(mask, 1.0, 0.0).astype(BF)


def down_lanes(row):
    return jnp.transpose(jnp.broadcast_to(row, (TILE, TILE)))


def sigmoid(v):
    return 0.5 * jnp.tanh(0.5 * v) + 0.5


def pad_rows(v, total=TILE):
    return jnp.concatenate([v, jnp.zeros((total - v.shape[0], v.shape[1]), v.dtype)], axis=0)


def sum_slots(ref, count):
    total = ref[0]
    for slot in range(1, count):
        total = total + ref[slot]
    return total


def step_kernel(
    sizes, packed,
    x_in, cot_in, mw_in, mb_in, nw_in, nb_in, cnt_ref, fe_in, fs_in, pm_in, ce_in, tm_in, te_in,
    out_to, ngrad_to, par_to,
    x_ref, cot_ref, mw_ref, mb_ref, nw_ref, nb_ref, fe_ref, fs_ref, pm_ref, ce_ref, tm_ref, te_ref,
    out_ref, ngrad_ref, par_ref, lsem,
    sums_r, kept, gat, sca, hl, slope, msgs, act_slope, hidden, aggf, pool_t, pool_l,
    gcat, gcat_t, o_top, l_top, sc_top, te_s, pos_s, key_s,
    sendbuf, halo, e0s, e0r, e0d, e0dr, e0u, e0ur, e1s, e1r, pss, psr, psd, psdr, psu, psur, tss, tsr,
    cb1, tab1, cb2, tab2, ths, thr, cfs, cfr, gts, gtr, rgs, rgr, rus, rur, rdr, bgs, bgr,
    f_cs, f_cr, f_xs, f_xr, f_zr, f_g,
    a_cs, a_cr, a_xs, a_xr, a_zr, a_g,
    ssem, rsem,
):
    X, Z, Y, C, nf, ne, nc, nec, nrow = sizes
    DOM = Z * Y * C
    NP = X * DOM
    halo_n = 64
    ext_n = nf + 2 * halo_n
    rim = nc // 8
    gx = lax.axis_index("grp")
    dm = lax.axis_index("dom")
    p = gx * DOM + dm
    z = lax.div(dm, Y * C)
    y = lax.rem(lax.div(dm, C), Y)
    c = lax.rem(dm, C)
    xz = gx * Z + z
    up = lax.rem(p + 1, NP)
    dn = lax.rem(p + NP - 1, NP)
    has_dn = p > 0
    has_up = p < NP - 1
    up2 = lax.rem(p + 2, NP)
    dn2 = lax.rem(p + NP - 2, NP)
    has_dn2 = p > 1
    has_up2 = p < NP - 2
    XY = X * Y
    ZC = Z * C
    xy = gx * Y + y
    zc = z * C + c

    def spot_of(q):
        return (lax.div(q, DOM), lax.rem(q, DOM))

    def plane(q):
        return (lax.div(q, Y), z * (Y * C) + lax.rem(q, Y) * C + c)

    def column(q):
        return (gx, lax.div(q, C) * (Y * C) + y * C + lax.rem(q, C))

    up_dev, dn_dev, up2_dev, dn2_dev = spot_of(up), spot_of(dn), spot_of(up2), spot_of(dn2)
    core_dev = (gx, dm + 1 - 2 * c)
    plane_devs = [plane(lax.rem(xy + d, XY)) for d in range(1, XY)]
    column_devs = [column(lax.rem(zc + d, ZC)) for d in range(1, ZC)]
    z_devs = [column(lax.rem(zc + d * C, ZC)) for d in range(1, Z)]

    loads = {}
    for spot, (name, src, dst) in enumerate(
        (
            ("fs", fs_in, fs_ref), ("x", x_in, x_ref), ("pm", pm_in, pm_ref), ("cot", cot_in, cot_ref),
            ("tm", tm_in, tm_ref), ("fe", fe_in, fe_ref), ("mw", mw_in, mw_ref), ("mb", mb_in, mb_ref),
            ("ce", ce_in, ce_ref), ("te", te_in, te_ref), ("nw", nw_in, nw_ref), ("nb", nb_in, nb_ref),
        )
    ):
        loads[name] = pltpu.make_async_copy(src, dst, lsem.at[spot])
        loads[name].start()
    barrier = pltpu.get_barrier_semaphore()
    partners = [up_dev, dn_dev, up2_dev, dn2_dev] + plane_devs + column_devs
    for dev in partners:
        pl.semaphore_signal(barrier, inc=1, device_id=dev, device_id_type=MESH)

    started = []

    def send(src, dst, dev):
        spot = len(started)
        copy = pltpu.make_async_remote_copy(
            src_ref=src, dst_ref=dst, send_sem=ssem.at[spot], recv_sem=rsem.at[spot],
            device_id=dev, device_id_type=MESH,
        )
        copy.start()
        started.append(copy)
        return copy

    def arrived(copies):
        for copy in copies:
            copy.wait_recv()

    ntile = ne // TILE
    ctile = nec // TILE
    lane = iota((TILE, TILE), 1)
    sub = iota((TILE, TILE), 0)
    ones = jnp.ones((TILE, TILE), BF)

    loads["fs"].wait()
    loads["x"].wait()
    send_row = jnp.concatenate([fs_ref[0, 0:1, :], fs_ref[0, 1:2, :]], axis=1)
    send_lanes = down_lanes(send_row)
    picks = jnp.concatenate([hot(send_lanes == lane + g * TILE) for g in range(nf // TILE)], axis=1)
    sendbuf[...] = mm(picks, x_ref[...]).astype(BF)
    pl.semaphore_wait(barrier, len(partners))
    halo_in = [
        send(sendbuf.at[halo_n : 2 * halo_n], halo.at[0:halo_n], up_dev),
        send(sendbuf.at[0:halo_n], halo.at[halo_n : 2 * halo_n], dn_dev),
    ]

    loads["pm"].wait()
    loads["cot"].wait()
    loads["tm"].wait()
    live = cnt_ref[0]
    alive = jnp.where(iota((nf, W), 0) < live, 1.0, 0.0)
    for g in range(nf // TILE):
        keys = pm_ref[0:1, g * TILE : (g + 1) * TILE]
        pool_t[:, g * TILE : (g + 1) * TILE] = hot((sub == keys) & (lane + g * TILE < live))
        pool_l[g * TILE : (g + 1) * TILE, :] = hot((down_lanes(keys) == lane) & (sub + g * TILE < live))
    gout = cot_ref[...] * alive
    counts = mm(pool_t[...], jnp.ones((nf, W), BF))
    lift = fold(mm(pool_t[...], wide(gout)))
    e0s[0:nc, :] = lift[nc:]
    e0s[nc : 2 * nc + rim, :] = jnp.concatenate([counts[nc:], counts[nc - rim : nc]], axis=0)
    e0d[...] = counts[:nc]
    e0u[...] = counts[2 * nc - rim :]
    e0_in = [send(e0s, e0r, up_dev), send(e0d, e0dr, dn_dev), send(e0u, e0ur, up2_dev)]
    rel = lax.rem(tm_ref[...] - (p - 1) * ROWS + NP * ROWS, NP * ROWS)
    rel = jnp.concatenate([rel, jnp.full((1, TILE - nc), -1, I32)], axis=1)
    top_t = hot(sub == rel)
    top_l = hot(down_lanes(rel) == lane)
    top_counts = mm(top_t, ones)

    loads["fe"].wait()

    def build(k, carry):
        at = pl.ds(pl.multiple_of(k * TILE, TILE), TILE)
        src, tgt = fe_ref[0, 0:1, at], fe_ref[0, 1:2, at]
        src_lanes, tgt_lanes = down_lanes(src), down_lanes(tgt)
        for g in range(ext_n // TILE):
            gat[at, g * TILE : (g + 1) * TILE] = hot(src_lanes == lane + g * TILE)
            sca[g * TILE : (g + 1) * TILE, at] = hot(sub + g * TILE == src)
        for g in range(nf // TILE):
            gat[at, ext_n + g * TILE : ext_n + (g + 1) * TILE] = hot(tgt_lanes == lane + g * TILE)
            sca[ext_n + g * TILE : ext_n + (g + 1) * TILE, at] = hot(sub + g * TILE == tgt)
        return carry

    lax.fori_loop(0, ntile, build, 0)
    loads["mw"].wait()
    loads["mb"].wait()
    ws0, wt0 = mw_ref[0, :W, :], mw_ref[0, W:, :]
    hl[0:nf, :] = wide(mm(x_ref[...], ws0))
    hl[ext_n : ext_n + nf, :] = wide(mm(x_ref[...], wt0) + mb_ref[0:1, :])

    loads["ce"].wait()
    for k in range(ctile):
        src = ce_ref[0, 0:1, k * TILE : (k + 1) * TILE]
        tgt = ce_ref[0, 1:2, k * TILE : (k + 1) * TILE]
        gcat[k * TILE : (k + 1) * TILE, 0:TILE] = hot(down_lanes(src) == lane)
        gcat[k * TILE : (k + 1) * TILE, TILE:] = hot(down_lanes(tgt) == lane)
        gcat_t[0:TILE, k * TILE : (k + 1) * TILE] = hot(sub == src)
        gcat_t[TILE:, k * TILE : (k + 1) * TILE] = hot(sub == tgt)

    first = p * ROWS
    loads["te"].wait()
    loads["nw"].wait()
    loads["nb"].wait()
    te_s[...] = jnp.full(te_s.shape, -1, I32)

    def lay(r, carry):
        at = pl.ds(pl.multiple_of(r * TILE, TILE), TILE)
        te_s[pl.ds(r, 1), :] = te_ref[0:1, at]
        te_s[pl.ds(TILE + r, 1), :] = te_ref[1:2, at]
        return carry

    lax.fori_loop(0, nrow, lay, 0)

    def owned(values):
        return (values >= first) & (values < first + ROWS)

    def keys_of(src, tgt):
        return (src * (NP * ROWS) + tgt + 1).astype(F32)

    def ends(key):
        code = key.astype(I32) - 1
        empty = code < 0
        return (
            jnp.where(empty, -1, lax.div(code, NP * ROWS)),
            jnp.where(empty, -1, lax.rem(code, NP * ROWS)),
        )

    half = ZC * ROWS // 2

    def place(node):
        part = lax.div(node, ROWS)
        core = lax.rem(part, C)
        py = lax.rem(lax.div(part, C), Y)
        pz = lax.rem(lax.div(part, C * Y), Z)
        px = lax.div(part, C * Y * Z)
        inner = (pz * C + core) * ROWS + lax.rem(node, ROWS)
        spot = lax.div(inner, half) * (XY * half) + (px * Y + py) * half + lax.rem(inner, half)
        return jnp.where(node < 0, -1, spot)

    near = jnp.where(lane < ROWS, lane + first, -2)
    near_t = jnp.where(sub < ROWS, sub + first, -2)

    def fill(t_lanes, s_lanes):
        (t_src, t_tgt), (s_src, s_tgt) = ends(t_lanes), ends(s_lanes)
        t_far, s_far = place(t_src), place(s_tgt)
        for g in range(NP * ROWS // TILE):
            o_top[0:TILE, g * TILE : (g + 1) * TILE] = hot(t_far == lane + g * TILE)
            o_top[TILE:, g * TILE : (g + 1) * TILE] = hot(s_far == lane + g * TILE)
        l_top[0:TILE, :] = hot(t_tgt == near)
        l_top[TILE:, :] = hot(s_src == near)
        sc_top[0:TILE, :] = hot(ends(jnp.transpose(t_lanes))[1] == near_t)
        sc_top[TILE:, :] = hot(ends(jnp.transpose(s_lanes))[0] == near_t)

    def fill_row(r):
        src, tgt = te_s[pl.ds(r, 1), :], te_s[pl.ds(TILE + r, 1), :]
        key = keys_of(src, tgt)
        fill(
            down_lanes(jnp.where(owned(tgt), key, 0.0)), down_lanes(jnp.where(owned(src), key, 0.0))
        )

    if packed:
        upper_ones = hot(sub <= lane)
        lower_ones = hot(lane < sub)
        sub_f = sub.astype(F32)
        key_s[...] = keys_of(te_s[0:TILE, :], te_s[TILE:, :])
        lists = []
        for values in (te_s[TILE:, :], te_s[0:TILE, :]):
            mine = owned(values)
            flags = hot(mine)
            offset = mm(lower_ones, mm(flags, ones).astype(BF))
            pos_s[...] = jnp.where(mine, mm(flags, upper_ones) + offset - 1.0, -1.0)

            def pick(r, acc):
                at = pl.ds(pl.multiple_of(r * 8, 8), 8)
                places, keys8 = pos_s[at, :], key_s[at, :]
                for i in range(8):
                    acc = acc + jnp.where(places[i : i + 1, :] == sub_f, keys8[i : i + 1, :], 0.0)
                return acc

            acc = lax.fori_loop(0, -(-nrow // 8), pick, jnp.zeros((TILE, TILE), F32))
            lists.append(jnp.broadcast_to(jnp.sum(acc, axis=1, keepdims=True), (TILE, TILE)))
        fill(*lists)

    arrived(e0_in)
    lower = jnp.where(has_dn, e0r[0 : 2 * nc, :], 0.0)
    grad_coarse0 = lift[:nc] + lower[:nc]
    den = jnp.maximum(counts[:nc] + lower[nc:], 1.0)
    den_up = jnp.maximum(e0dr[...] + counts[nc:], 1.0)
    den_dn = jnp.maximum(e0r[2 * nc :, :] + jnp.where(has_dn2, e0ur[...], 0.0), 1.0)
    top_g = fold(mm(top_t, pad_rows(wide(grad_coarse0))))
    e1s[0, 0:ROWS, :] = top_counts[0:ROWS]
    e1s[0, ROWS:, :] = top_g[0:ROWS]
    e1s[1, 0:ROWS, :] = top_counts[2 * ROWS : 3 * ROWS]
    e1s[1, ROWS:, :] = top_g[2 * ROWS : 3 * ROWS]
    e1_in = [send(e1s.at[0], e1r.at[0], dn_dev), send(e1s.at[1], e1r.at[1], up_dev)]

    arrived(halo_in)
    halo_rows = sub
    live_halo = (has_dn & (halo_rows < halo_n)) | (has_up & (halo_rows >= halo_n))
    halo_f = jnp.where(live_halo, halo[...].astype(F32), 0.0).astype(BF)
    hl[nf:ext_n, :] = wide(mm(halo_f, ws0))
    step = 4 * TILE

    def forward(k, carry):
        at = pl.ds(pl.multiple_of(k * step, step), step)
        pre = fold(mm(gat[at, :], hl[...]))
        s = sigmoid(pre)
        slope[at, :] = s * (1.0 + pre * (1.0 - s))
        msgs[at, :] = wide(pre * s)
        return carry

    lax.fori_loop(0, ne // step, forward, 0)

    def node_forward(rows, agg, level):
        act = mm(rows, nw_ref[level, :W, :]) + mm(agg, nw_ref[level, W:, :]) + nb_ref[level : level + 1, :]
        s = sigmoid(act)
        return (rows.astype(F32) + act * s).astype(BF), s * (1.0 + act * (1.0 - s))

    def node_backward(rows, agg, act_slopes, grad, level):
        g_act = grad * act_slopes
        low = g_act.astype(BF)
        pair = nt(low, nw_ref[level])
        return (
            grad + pair[:, :W],
            pair[:, W:].astype(BF),
            tn(rows, low),
            tn(agg, low),
            jnp.sum(g_act, axis=0, keepdims=True),
        )

    for k in range(nf // step):
        at = slice(k * step, (k + 1) * step)
        agg = fold(mm(sca[ext_n + k * step : ext_n + (k + 1) * step, :], msgs[...])).astype(BF)
        new, act_s = node_forward(x_ref[at, :], agg, 0)
        aggf[at, :] = agg
        hidden[at, :] = new
        act_slope[at, :] = act_s

    pooled = mm(pool_t[...], hidden[...])
    pss[...] = pooled[nc - rim :]
    psd[...] = pooled[:rim]
    psu[...] = pooled[2 * nc - rim :]
    ps_in = [send(pss, psr, up_dev), send(psd, psdr, dn_dev), send(psu, psur, up2_dev)]
    arrived(e1_in)
    own_win = slice(ROWS, 2 * ROWS)
    top_den = jnp.maximum(top_counts[own_win] + e1r[0, 0:ROWS, :] + e1r[1, 0:ROWS, :], 1.0)
    top_grad = pad_rows(top_g[own_win] + e1r[0, ROWS:, :] + e1r[1, ROWS:, :])
    arrived(ps_in)
    start_f = ((pooled[:nc] + jnp.where(has_dn, psr[rim:, :], 0.0)) / den).astype(BF).astype(F32)
    left = (psr[0:rim, :] + jnp.where(has_dn2, psur[...], 0.0)) / den_dn
    right = (psdr[...] + pooled[nc : nc + rim]) / den_up[:rim]
    start_p = pad_rows(start_f).astype(BF)
    ws1, wt1 = mw_ref[1, :W, :], mw_ref[1, W:, :]
    near_part = wide(mm(start_p, wt1) + mb_ref[1:2, :])
    cext = pad_rows(
        jnp.concatenate(
            [jnp.where(has_dn, left, 0.0), start_f, jnp.where(has_up, right, 0.0)], axis=0
        )
    ).astype(BF)
    pre = fold(mm(gcat[...], jnp.concatenate([wide(mm(cext, ws1)), near_part], axis=0)))
    s = sigmoid(pre)
    slope_c = s * (1.0 + pre * (1.0 - s))
    agg_c = fold(mm(gcat_t[TILE:, :], wide(pre * s))).astype(BF)
    c_hidden, act_slope_c = node_forward(start_p, agg_c, 1)
    keep = sub < nc
    c_hidden_f = jnp.where(keep, c_hidden.astype(F32), 0.0)
    top_part = mm(top_t, c_hidden_f.astype(BF))
    tss[0] = top_part[0:ROWS]
    tss[1] = top_part[2 * ROWS : 3 * ROWS]
    ts_in = [send(tss.at[0], tsr.at[0], dn_dev), send(tss.at[1], tsr.at[1], up_dev)]
    arrived(ts_in)
    top_start = ((top_part[own_win] + tsr[0] + tsr[1]) / top_den).astype(BF)

    def gather(own, cb, tab):
        cb[zc] = own
        copies = [send(cb.at[zc], cb.at[zc], dev) for dev in column_devs]
        yield
        arrived(copies)
        tab[c, xy] = cb[pl.ds(c * (ZC // 2), ZC // 2)].reshape(half, W).astype(BF)
        copies = [send(tab.at[c, xy], tab.at[c, xy], dev) for dev in plane_devs]
        yield
        arrived(copies)
        copies = [send(tab.at[c], tab.at[c], core_dev)]
        yield
        arrived(copies)

    for _ in gather(top_start.astype(F32), cb1, tab1):
        pass

    ws2, wt2, mb2 = mw_ref[2, :W, :], mw_ref[2, W:, :], mb_ref[2:3, :]
    top_rows = pad_rows(top_start.astype(F32)).astype(BF)
    kept[:, 0:W] = top_rows

    def t_edges():
        far = mm(o_top[0:TILE, :], tab1[...].reshape(NP * ROWS, W)).astype(BF)
        close = mm(l_top[0:TILE, :], kept[:, 0:W]).astype(BF)
        pre_t = mm(far, ws2) + mm(close, wt2) + mb2
        s = sigmoid(pre_t)
        return far, close, pre_t * s, s * (1.0 + pre_t * (1.0 - s))

    def t_sums(message):
        return fold(mm(sc_top[0:TILE, :], wide(message)))

    def t_back(far, close, slope_t):
        g_pre_t = mm(l_top[0:TILE, :], kept[:, W:]) * slope_t
        low_t = g_pre_t.astype(BF)
        return (
            tn(far, low_t),
            tn(close, low_t),
            mm(sc_top[0:TILE, :], low_t),
            jnp.sum(g_pre_t, axis=0, keepdims=True),
        )

    def s_slopes():
        far = mm(o_top[TILE:, :], tab1[...].reshape(NP * ROWS, W)).astype(BF)
        close = mm(l_top[TILE:, :], kept[:, 0:W]).astype(BF)
        pre_s = mm(close, ws2) + mm(far, wt2) + mb2
        s = sigmoid(pre_s)
        return s * (1.0 + pre_s * (1.0 - s))

    def s_back(slope_s):
        g_far = mm(o_top[TILE:, :], tab2[...].reshape(NP * ROWS, W))
        return mm(sc_top[TILE:, :], (g_far * slope_s).astype(BF))

    def over_rows(work):
        sums_r[...] = jnp.zeros(sums_r.shape, F32)

        def one(r, carry):
            fill_row(r)
            for spot, term in enumerate(work()):
                sums_r[spot, 0 : term.shape[0], :] += term
            return carry

        lax.fori_loop(0, nrow, one, 0)

    def t_back_row():
        far = mm(o_top[0:TILE, :], tab1[...].reshape(NP * ROWS, W)).astype(BF)
        both = mm(l_top[0:TILE, :], kept[...])
        close = both[:, 0:W].astype(BF)
        pre_t = mm(far, ws2) + mm(close, wt2) + mb2
        s = sigmoid(pre_t)
        g_pre_t = both[:, W:] * (s * (1.0 + pre_t * (1.0 - s)))
        low_t = g_pre_t.astype(BF)
        return (
            tn(far, low_t),
            tn(close, low_t),
            mm(sc_top[0:TILE, :], low_t),
            jnp.sum(g_pre_t, axis=0, keepdims=True),
        )

    if packed:
        t_far_rows, t_close_rows, message, slope_t = t_edges()
        agg_t = t_sums(message).astype(BF)
    else:
        over_rows(lambda: (t_sums(t_edges()[2]),))
        agg_t = sums_r[0].astype(BF)
    t_hidden, act_slope_t = node_forward(top_rows, agg_t, 2)
    g_nodes, g_agg, dwn2_a, dwn2_b, dbn2 = node_backward(top_rows, agg_t, act_slope_t, top_grad, 2)
    kept[:, W:] = g_agg
    key_s[...] = g_nodes
    a_cs[1, 2 * W : 3 * W, :] = dwn2_a
    a_cs[1, 3 * W : 4 * W, :] = dwn2_b
    second = gather(g_agg.astype(F32)[:ROWS], cb2, tab2)
    next(second)
    own_hidden = t_hidden.astype(F32)[:ROWS]
    ths[...] = own_hidden
    th_in = [send(ths, thr.at[0], dn_dev), send(ths, thr.at[1], up_dev)]
    if packed:
        slope_s = s_slopes()
        backs = t_back(t_far_rows, t_close_rows, slope_t)
    else:
        over_rows(t_back_row)
        backs = sums_r[0], sums_r[1], sums_r[2], sums_r[3, 0:1, :]
    dwm2_a, dwm2_b, sums_t, dbm2 = backs
    a_half = a_cs.shape[1] - ROWS
    a_cs[1, 0:W, :] = dwm2_a
    a_cs[1, W : 2 * W, :] = dwm2_b
    g_nodes = key_s[...] + nt_split(sums_t, wt2)
    next(second)
    arrived(th_in)
    window = pad_rows(jnp.concatenate([thr[1], own_hidden, thr[0]], axis=0)).astype(BF)
    final = (c_hidden_f + mm(top_l, window)).astype(BF)[:nc]
    cfs[...] = final
    cf_in = [send(cfs, cfr, dn_dev)]
    arrived(cf_in)
    lift_rows = jnp.concatenate([final, cfr[...]], axis=0)
    lifted = mm(pool_l[...], lift_rows)
    out_ref[...] = ((hidden[...].astype(F32) + lifted) * alive).astype(BF)
    stores = [pltpu.make_async_copy(out_ref, out_to, lsem.at[12])]
    stores[0].start()
    for _ in second:
        pass

    if packed:
        sums_s = s_back(slope_s)
    else:
        over_rows(lambda: (s_back(s_slopes()),))
        sums_s = sums_r[0]
    g_nodes = g_nodes + nt_split(sums_s, ws2)
    g_own = g_nodes[:ROWS] / top_den
    gts[...] = g_own
    gt_in = [send(gts, gtr.at[0], dn_dev), send(gts, gtr.at[1], up_dev)]
    arrived(gt_in)
    window = pad_rows(jnp.concatenate([gtr[1], g_own, gtr[0]], axis=0))
    grad_coarse = pad_rows(grad_coarse0) + fold(mm(top_l, wide(window)))

    g_nodes, g_agg, dwn1_a, dwn1_b, dbn1 = node_backward(start_p, agg_c, act_slope_c, grad_coarse, 1)
    g_pre = mm(gcat[:, TILE:], g_agg) * slope_c
    dbm1 = jnp.sum(g_pre, axis=0, keepdims=True)
    sums = mm(gcat_t[...], g_pre.astype(BF))
    g_ext = nt_split(sums[:TILE], ws1)
    g_start = (g_nodes + nt_split(sums[TILE:], wt1))[:nc] + g_ext[rim : rim + nc]
    rgs[0:nc, :] = g_start
    rgs[nc:, :] = g_ext[:rim]
    rus[...] = g_ext[rim + nc : 2 * rim + nc]
    rg_in = [
        send(rgs, rgr, dn_dev),
        send(rus, rur, up_dev),
        send(rgs.at[nc : nc + rim], rdr, dn2_dev),
    ]
    a_cs[0, 0:W, :] = fold(tn(cext, wide(sums[:TILE])))
    a_cs[0, W : 2 * W, :] = fold(tn(start_p, wide(sums[TILE:])))
    a_cs[0, 2 * W : 3 * W, :] = dwn1_a
    a_cs[0, 3 * W : 4 * W, :] = dwn1_b
    a_bias = jnp.concatenate([dbm1, dbn1, dbm2, dbn2, jnp.zeros((4, W), F32)], axis=0)
    a_cs[0, a_half:, :] = a_bias
    a_cs[1, a_half:, :] = a_bias

    scale = 1.0 / float(nf * NP) ** 0.5

    def reduce(cs, cr, xs, xr, zr, g, biases):
        copies = [send(cs.at[1 - c], cr, core_dev)]
        yield
        arrived(copies)
        part = cs[c] + cr[...]
        n = g.shape[2]
        for j in range(XY):
            xs[j, 0:n, :] = part[j * n : (j + 1) * n]
            xs[j, n:, :] = part[XY * n :]
        copies = [
            send(xs.at[lax.rem(xy + d + 1, XY)], xr.at[xy], dev) for d, dev in enumerate(plane_devs)
        ]
        xr[xy] = xs[xy]
        yield
        arrived(copies)
        zr[z] = sum_slots(xr, XY)
        copies = [send(zr.at[z], zr.at[z], dev) for dev in z_devs]
        yield
        arrived(copies)
        part = sum_slots(zr, Z) * scale
        biases.append(part[n:])
        g[c, xy] = part[:n]
        copies = [send(g.at[c, xy], g.at[c, xy], dev) for dev in plane_devs]
        yield
        arrived(copies)
        copies = [send(g.at[c], g.at[c], core_dev)]
        yield
        arrived(copies)

    a_bias_out, f_bias_out = [], []
    reduce_a = reduce(a_cs, a_cr, a_xs, a_xr, a_zr, a_g, a_bias_out)
    next(reduce_a)
    arrived(rg_in)
    middle = jnp.zeros((nc - 2 * rim, W), F32)
    g_csum = (
        g_start
        + jnp.concatenate(
            [jnp.where(has_dn, rur[...], 0.0), middle, jnp.where(has_up, rgr[nc:, :], 0.0)], axis=0
        )
    ) / den
    upper = (
        rgr[0:nc, :] + jnp.concatenate([rus[...], middle, jnp.where(has_up2, rdr[...], 0.0)], axis=0)
    ) / den_up
    pool_grad = jnp.concatenate([g_csum, jnp.where(has_up, upper, 0.0)], axis=0)
    next(reduce_a)
    grad_fine = gout + fold(mm(pool_l[...], wide(pool_grad)))

    g_nodes, g_agg, dwn0_a, dwn0_b, dbn0 = node_backward(x_ref[...], aggf[...], act_slope[...], grad_fine, 0)
    aggf[...] = g_agg
    f_cs[1, 0:W, :] = dwn0_a
    f_cs[1, W : 2 * W, :] = dwn0_b

    def backward(k, total):
        at = pl.ds(pl.multiple_of(k * step, step), step)
        g_pre = mm(gat[at, ext_n:], aggf[...]) * slope[at, :]
        msgs[at, 0:W] = g_pre.astype(BF)
        return total + jnp.sum(g_pre, axis=0, keepdims=True)

    dbm0 = lax.fori_loop(0, ne // step, backward, jnp.zeros((1, W), F32))
    sums_h = mm(sca[nf:ext_n, :], msgs[:, 0:W])
    bgs[...] = nt_split(sums_h, ws0).astype(BF)
    bg_in = [
        send(bgs.at[0:halo_n], bgr.at[halo_n : 2 * halo_n], dn_dev),
        send(bgs.at[halo_n : 2 * halo_n], bgr.at[0:halo_n], up_dev),
    ]
    sums_s = mm(sca[0:nf, :], msgs[:, 0:W])
    sums_t = mm(sca[ext_n:, :], msgs[:, 0:W])
    f_cs[0, 0:W, :] = fold(tn(x_ref[...], wide(sums_s)) + tn(halo_f, wide(sums_h)))
    f_cs[0, W : 2 * W, :] = fold(tn(x_ref[...], wide(sums_t)))
    f_bias = jnp.concatenate([dbm0, dbn0, jnp.zeros((6, W), F32)], axis=0)
    f_half = f_cs.shape[1] - ROWS
    f_cs[0, f_half:, :] = f_bias
    f_cs[1, f_half:, :] = f_bias
    reduce_f = reduce(f_cs, f_cr, f_xs, f_xr, f_zr, f_g, f_bias_out)
    next(reduce_f)
    next(reduce_a)
    node_grad = g_nodes + nt_split(sums_s, ws0) + nt_split(sums_t, wt0)
    arrived(bg_in)
    live_back = (has_dn & (sub < halo_n)) | (has_up & (sub >= halo_n))
    back = jnp.where(live_back, bgr[...].astype(F32), 0.0).astype(BF)
    for g in range(nf // TILE):
        at = slice(g * TILE, (g + 1) * TILE)
        ngrad_ref[at, :] = node_grad[at] + mm(hot(sub + g * TILE == send_row), back)
    stores.append(pltpu.make_async_copy(ngrad_ref, ngrad_to, lsem.at[13]))
    stores[1].start()
    pending = [reduce_f, reduce_a]
    while pending:
        for item in list(pending):
            if next(item, 0) == 0:
                pending.remove(item)

    for copy in started:
        copy.wait_send()
    par_ref[0 : 4 * W, :] = f_g[...].reshape(4 * W, W)
    par_ref[4 * W : 12 * W, :] = a_g[...].reshape(8 * W, W)
    par_ref[12 * W : 12 * W + 8, :] = f_bias_out[0]
    par_ref[12 * W + 8 :, :] = a_bias_out[0]
    stores.append(pltpu.make_async_copy(par_ref, par_to, lsem.at[14]))
    stores[2].start()
    for copy in stores:
        copy.wait()


def parts_kernel(
    out_in, grad_in, par_in, out_to, grad_to, mw_to, mb_to, nw_to, nb_to, out, grad, par, mb, nb, sem
):
    moves = [(out_in, out, out_to), (grad_in, grad, grad_to)]
    for level in range(3):
        at = 4 * W * level
        for first, to in ((at, mw_to), (at + 2 * W, nw_to)):
            rows = slice(first, first + 2 * W)
            moves.append((par_in.at[rows, :], par.at[rows, :], to.at[level]))
    tail = slice(12 * W, 12 * W + 16)
    bias = pltpu.make_async_copy(par_in.at[tail, :], par.at[tail, :], sem.at[16])
    bias.start()
    loads = [pltpu.make_async_copy(src, mid, sem.at[i]) for i, (src, mid, _) in enumerate(moves)]
    for copy in loads:
        copy.start()
    stores = [pltpu.make_async_copy(mid, dst, sem.at[8 + i]) for i, (_, mid, dst) in enumerate(moves)]
    bias.wait()
    f_bias, a_bias = par[12 * W : 12 * W + 8, :], par[12 * W + 8 :, :]
    mb[...] = jnp.concatenate([f_bias[0:1], a_bias[0:1], a_bias[2:3]], axis=0)
    nb[...] = jnp.concatenate([f_bias[1:2], a_bias[1:2], a_bias[3:4]], axis=0)
    stores.append(pltpu.make_async_copy(mb, mb_to, sem.at[17]))
    stores.append(pltpu.make_async_copy(nb, nb_to, sem.at[18]))
    stores[8].start()
    stores[9].start()
    for load, store in zip(loads, stores):
        load.wait()
        store.start()
    for copy in stores:
        copy.wait()


def one_step(split, packed, *args):
    (fine_nodes, cotangent, msg_weights, msg_biases, node_weights, node_biases, node_count,
     fine_edges, fine_send, pool_map, coarse_edges, top_map, top_edges) = args
    Z, Y, C = split
    X = lax.axis_size("grp")
    NP = X * Z * Y * C
    nf = fine_nodes.shape[0]
    ne, nec, et = fine_edges.shape[2], coarse_edges.shape[2], top_edges.shape[1]
    nc = top_map.shape[1]
    vm = lambda *shape: pltpu.VMEM(shape, F32)
    vb = lambda *shape: pltpu.VMEM(shape, BF)
    ext_n = nf + 128
    gathers = [vm(Z * C, ROWS, W), vb(2, X * Y, Z * C * ROWS // 2, W)]

    def reduce_bufs(total):
        r = total // 2 // X // Y
        return [
            vm(2, total // 2 + ROWS, W),
            vm(total // 2 + ROWS, W),
            vm(X * Y, r + ROWS, W),
            vm(X * Y, r + ROWS, W),
            vm(Z, r + ROWS, W),
            vm(2, X * Y, r, W),
        ]

    loaded = args[:6] + args[7:]
    outs = [
        jax.ShapeDtypeStruct((nf, W), BF),
        jax.ShapeDtypeStruct((nf, W), F32),
        jax.ShapeDtypeStruct((12 * W + 16, W), F32),
    ]
    scratch = [pltpu.VMEM(a.shape, a.dtype) for a in [*loaded, *outs]]
    scratch += [
        pltpu.SemaphoreType.DMA((15,)),
        vm(4, TILE, W), vb(TILE, 2 * W),
        vb(ne, ext_n + nf), vb(ext_n + nf, ne), vb(ext_n + nf, 2 * W), vm(ne, W), vb(ne, 2 * W),
        vm(nf, W), vb(nf, W), vb(nf, W), vb(TILE, nf), vb(nf, TILE),
        vb(nec, 2 * TILE), vb(2 * TILE, nec), vb(2 * TILE, NP * ROWS), vb(2 * TILE, TILE),
        vb(2 * TILE, TILE), pltpu.VMEM((2 * TILE, TILE), I32), vm(TILE, TILE), vm(TILE, TILE),
        vb(128, W), vb(128, W), vm(2 * nc + 8, W), vm(2 * nc + 8, W), vm(nc, W), vm(nc, W),
        vm(8, W), vm(8, W), vm(2, 16, W), vm(2, 16, W),
        vm(nc + 8, W), vm(nc + 8, W), vm(8, W), vm(8, W), vm(8, W), vm(8, W),
        vm(2, 8, W), vm(2, 8, W),
        *gathers, *gathers,
        vm(8, W), vm(2, 8, W), vb(nc, W), vb(nc, W), vm(8, W), vm(2, 8, W),
        vm(nc + 8, W), vm(nc + 8, W), vm(8, W), vm(8, W), vm(8, W), vb(128, W), vb(128, W),
        *reduce_bufs(4 * W), *reduce_bufs(8 * W),
    ]
    copies = 24 + 2 * (X * Y + Z * C) + 2 * (2 * X * Y + Z)
    scratch += [pltpu.SemaphoreType.DMA((copies,)), pltpu.SemaphoreType.DMA((copies,))]
    in_hbm = pl.BlockSpec(memory_space=pltpu.HBM)
    sizes = (X, Z, Y, C, nf, ne, nc, nec, et // TILE)
    return pl.pallas_call(
        functools.partial(step_kernel, sizes, packed),
        out_shape=outs,
        in_specs=[in_hbm] * 6 + [pl.BlockSpec(memory_space=pltpu.SMEM)] + [in_hbm] * 6,
        out_specs=[in_hbm] * 3,
        scratch_shapes=scratch,
        compiler_params=pltpu.CompilerParams(
            collective_id=0 if packed else 1, has_side_effects=True, vmem_limit_bytes=64 * 1024 * 1024
        ),
        name="step" if packed else "step_long",
    )(*args)


def per_device(split, *args):
    owner = args[-1] // ROWS
    digits = jnp.arange(16)[None, :, None]
    high = (owner[:, None, :] // 16 == digits).astype(BF)
    low = (owner[:, None, :] % 16 == digits).astype(BF)
    counts = jnp.einsum("khe,kle->khl", high, low, preferred_element_type=F32)
    outs = lax.cond(
        jnp.max(counts) <= CAP,
        functools.partial(one_step, split, True),
        functools.partial(one_step, split, False),
        *args,
    )
    in_hbm = pl.BlockSpec(memory_space=pltpu.HBM)
    like = [outs[0], outs[1], args[2], args[3], args[4], args[5]]
    types = [BF, F32, F32, F32, F32, F32]
    return tuple(
        pl.pallas_call(
            parts_kernel,
            out_shape=[jax.ShapeDtypeStruct(a.shape, t) for a, t in zip(like, types)],
            in_specs=[in_hbm] * 3,
            out_specs=[in_hbm] * 6,
            scratch_shapes=[
                *[pltpu.VMEM(a.shape, a.dtype) for a in outs],
                pltpu.VMEM((3, W), F32),
                pltpu.VMEM((3, W), F32),
                pltpu.SemaphoreType.DMA((19,)),
            ],
            name="parts",
        )(*outs)
    )


def solution(mesh):
    return jax.shard_map(
        functools.partial(per_device, DOM_SPLIT),
        mesh=mesh,
        in_specs=(
            P(("grp", "dom"), None),
            P(("grp", "dom"), None),
            P(),
            P(),
            P(),
            P(),
            P(("grp", "dom")),
            P(("grp", "dom"), None, None),
            P(("grp", "dom"), None, None),
            P(("grp", "dom"), None),
            P(("grp", "dom"), None, None),
            P(("grp", "dom"), None),
            P(),
        ),
        out_specs=(P(("grp", "dom"), None), P(("grp", "dom"), None), P(), P(), P(), P()),
        check_vma=False,
    )
```

profile of v0, /device:TPU:1, one launch (start us, length us, event | category | flops | bytes accessed | tf_op | source)
XLA Modules:
  0.0 108.4 jit_solution(18371554315204494932)
XLA Ops:
  0.6 1.3 %and_select_fusion.1 = (s32[2,12288]{1,0:T(2,128)S(1)}, s32[2,12288]{1,0:T(2,128)S(1)}) fusion(s32[2,12288]{1,0:T(2,128)} %param.27), kind=kLoop, calls=%fused_computation.7 | loop fusion | flops 737280 | bytes 294912 | tf_op jit(solution)/shard_map/jit(floor_divide)/jit(_where)/select_n | solution.py:762
  2.0 0.1 and_select_fusion
  2.1 1.2 %fusion.3 = f32[]{:T(128)} fusion(s32[2,12288]{1,0:T(2,128)S(1)} %and_select_fusion, s32[2,12288]{1,0:T(2,128)S(1)} %get-tuple-element.90), kind=kOutput, calls=%fused_computation.5 | convolution fusion | flops 13369855 | bytes 196612 | tf_op jit(solution)/shard_map/khe,kle->khl/dot_general | solution.py:764
  3.9 102.1 %conditional.1 = ((bf16[512,128]{1,0:T(8,128)(2,1)}, f32[512,128]{1,0:T(8,128)}, f32[1552,128]{1,0:T(8,128)})) conditional(s32[]{:T(128)} %convert_element_type.2, (bf16[512,128]{1,0:T(8,128)(2,1)}, f32[512,128]{1,0:T(8,128)}, bf16[3,256,128]{2,1,0:T(8,128)(2,1)}, f32[3,128]{1,0:T(4,128)}, bf16[3,256,128]{2,1,0:T(8,128)(2,1)}, ...), branch_computations={%region_1.2_spmd, %region_2.3_spmd} | conditional | bytes 8 | solution.py:765
  4.1 101.9 %step.1 = (bf16[512,128]{1,0:T(8,128)(2,1)}, f32[512,128]{1,0:T(8,128)}, f32[1552,128]{1,0:T(8,128)}) custom-call(bf16[512,128]{1,0:T(8,128)(2,1)} %get-tuple-element.65.x_in, f32[512,128]{1,0:T(8,128)} %get-tuple-element.66.cot_in, bf16[3,256,128]{2,1,0:T(8,128)(2,1)} %get-tuple-element.67.mw_in, f32[3,128]{1,0:T(4,128)} %get-tuple-element.68.mb_in, ...), custom_call_target="tpu_custom_call" | custom-call | tf_op jit(solution)/shard_map/cond/branch_1_fun/step/pallas_call | solution.py:746
  106.0 2.2 %parts.1 = (bf16[512,128]{1,0:T(8,128)(2,1)}, f32[512,128]{1,0:T(8,128)}, f32[3,256,128]{2,1,0:T(8,128)}, f32[3,128]{1,0:T(4,128)}, f32[3,256,128]{2,1,0:T(8,128)}, /*index=5*/f32[3,128]{1,0:T(4,128)}) custom-call(bf16[512,128]{1,0:T(8,128)(2,1)} %get-tuple-element.87.out_in, f32[512,128]{1,0:T(8,128)} %get-tuple-element.88.grad_in, ...), custom_call_target="tpu_custom_call" | custom-call | tf_op jit(solution)/shard_map/parts/pallas_call | solution.py:775
where the time goes:
time: 109 us; the launch traced here: 108 us
  Pallas kernels  104 us (95%)
  other arithmetic  1.48 us (1%)
  between operations  1.46 us (1%)
  matrix products  1.15 us (1%)
    pallas_call x1, Pallas kernels, one_step(): pl.pallas_call(functools.partial(step_kernel, sizes, packed), out_shape=o...  102 us

commit v1 on v0

--- a/solution.py
+++ b/solution.py
@@ -7,7 +7,7 @@
 from jax.experimental.pallas import tpu as pltpu
 from jax.sharding import PartitionSpec as P
 
-BF, F32, I32 = jnp.bfloat16, jnp.float32, jnp.int32
+BF, F32, I32, I16 = jnp.bfloat16, jnp.float32, jnp.int32, jnp.int16
 MESH = pl.DeviceIdType.MESH
 W = 128
 TILE = 128
@@ -48,6 +48,10 @@
 
 def hot(mask):
     return jnp.where(mask, 1.0, 0.0).astype(BF)
+
+
+def hot16(mask):
+    return jnp.where(mask, jnp.ones(mask.shape, BF), jnp.zeros(mask.shape, BF))
 
 
 def down_lanes(row):
@@ -77,7 +81,7 @@
     out_ref, ngrad_ref, par_ref, lsem,
     sums_r, kept, gat, sca, hl, slope, msgs, act_slope, hidden, aggf, pool_t, pool_l,
     gcat, gcat_t, o_top, l_top, sc_top, te_s, pos_s, key_s,
-    sendbuf, halo, e0s, e0r, e0d, e0dr, e0u, e0ur, e1s, e1r, pss, psr, psd, psdr, psu, psur, tss, tsr,
+    sendbuf, halo, lfs, lfr, e0s, e0r, e0d, e0dr, e0u, e0ur, e1s, e1r, pss, psr, psd, psdr, psu, psur, tss, tsr,
     cb1, tab1, cb2, tab2, ths, thr, cfs, cfr, gts, gtr, rgs, rgr, rus, rur, rdr, bgs, bgr,
     f_cs, f_cr, f_xs, f_xr, f_zr, f_g,
     a_cs, a_cr, a_xs, a_xr, a_zr, a_g,
@@ -174,40 +178,46 @@
     ]
 
     loads["pm"].wait()
-    loads["cot"].wait()
     loads["tm"].wait()
     live = cnt_ref[0]
     alive = jnp.where(iota((nf, W), 0) < live, 1.0, 0.0)
     for g in range(nf // TILE):
         keys = pm_ref[0:1, g * TILE : (g + 1) * TILE]
         pool_t[:, g * TILE : (g + 1) * TILE] = hot((sub == keys) & (lane + g * TILE < live))
-        pool_l[g * TILE : (g + 1) * TILE, :] = hot((down_lanes(keys) == lane) & (sub + g * TILE < live))
-    gout = cot_ref[...] * alive
     counts = mm(pool_t[...], jnp.ones((nf, W), BF))
-    lift = fold(mm(pool_t[...], wide(gout)))
-    e0s[0:nc, :] = lift[nc:]
-    e0s[nc : 2 * nc + rim, :] = jnp.concatenate([counts[nc:], counts[nc - rim : nc]], axis=0)
+    e0s[...] = jnp.concatenate([counts[nc:], counts[nc - rim : nc]], axis=0)
     e0d[...] = counts[:nc]
     e0u[...] = counts[2 * nc - rim :]
-    e0_in = [send(e0s, e0r, up_dev), send(e0d, e0dr, dn_dev), send(e0u, e0ur, up2_dev)]
     rel = lax.rem(tm_ref[...] - (p - 1) * ROWS + NP * ROWS, NP * ROWS)
     rel = jnp.concatenate([rel, jnp.full((1, TILE - nc), -1, I32)], axis=1)
     top_t = hot(sub == rel)
-    top_l = hot(down_lanes(rel) == lane)
     top_counts = mm(top_t, ones)
+    e1s[0, 0:ROWS, :] = top_counts[0:ROWS]
+    e1s[1, 0:ROWS, :] = top_counts[2 * ROWS : 3 * ROWS]
+    e0_in = [
+        send(e0s, e0r, up_dev),
+        send(e0d, e0dr, dn_dev),
+        send(e0u, e0ur, up2_dev),
+        send(e1s.at[0, 0:ROWS], e1r.at[0, 0:ROWS], dn_dev),
+        send(e1s.at[1, 0:ROWS], e1r.at[1, 0:ROWS], up_dev),
+    ]
 
     loads["fe"].wait()
+
+    lane16, sub16 = lane.astype(I16), sub.astype(I16)
 
     def build(k, carry):
         at = pl.ds(pl.multiple_of(k * TILE, TILE), TILE)
         src, tgt = fe_ref[0, 0:1, at], fe_ref[0, 1:2, at]
-        src_lanes, tgt_lanes = down_lanes(src), down_lanes(tgt)
+        src_lanes, tgt_lanes = down_lanes(src).astype(I16), down_lanes(tgt).astype(I16)
+        src16 = jnp.broadcast_to(src, (TILE, TILE)).astype(I16)
+        tgt16 = jnp.broadcast_to(tgt, (TILE, TILE)).astype(I16)
         for g in range(ext_n // TILE):
-            gat[at, g * TILE : (g + 1) * TILE] = hot(src_lanes == lane + g * TILE)
-            sca[g * TILE : (g + 1) * TILE, at] = hot(sub + g * TILE == src)
+            gat[at, g * TILE : (g + 1) * TILE] = hot16(src_lanes == lane16 + g * TILE)
+            sca[g * TILE : (g + 1) * TILE, at] = hot16(sub16 == (src16 - g * TILE))
         for g in range(nf // TILE):
-            gat[at, ext_n + g * TILE : ext_n + (g + 1) * TILE] = hot(tgt_lanes == lane + g * TILE)
-            sca[ext_n + g * TILE : ext_n + (g + 1) * TILE, at] = hot(sub + g * TILE == tgt)
+            gat[at, ext_n + g * TILE : ext_n + (g + 1) * TILE] = hot16(tgt_lanes == lane16 + g * TILE)
+            sca[ext_n + g * TILE : ext_n + (g + 1) * TILE, at] = hot16(sub16 == (tgt16 - g * TILE))
         return carry
 
     lax.fori_loop(0, ntile, build, 0)
@@ -216,112 +226,6 @@
     ws0, wt0 = mw_ref[0, :W, :], mw_ref[0, W:, :]
     hl[0:nf, :] = wide(mm(x_ref[...], ws0))
     hl[ext_n : ext_n + nf, :] = wide(mm(x_ref[...], wt0) + mb_ref[0:1, :])
-
-    loads["ce"].wait()
-    for k in range(ctile):
-        src = ce_ref[0, 0:1, k * TILE : (k + 1) * TILE]
-        tgt = ce_ref[0, 1:2, k * TILE : (k + 1) * TILE]
-        gcat[k * TILE : (k + 1) * TILE, 0:TILE] = hot(down_lanes(src) == lane)
-        gcat[k * TILE : (k + 1) * TILE, TILE:] = hot(down_lanes(tgt) == lane)
-        gcat_t[0:TILE, k * TILE : (k + 1) * TILE] = hot(sub == src)
-        gcat_t[TILE:, k * TILE : (k + 1) * TILE] = hot(sub == tgt)
-
-    first = p * ROWS
-    loads["te"].wait()
-    loads["nw"].wait()
-    loads["nb"].wait()
-    te_s[...] = jnp.full(te_s.shape, -1, I32)
-
-    def lay(r, carry):
-        at = pl.ds(pl.multiple_of(r * TILE, TILE), TILE)
-        te_s[pl.ds(r, 1), :] = te_ref[0:1, at]
-        te_s[pl.ds(TILE + r, 1), :] = te_ref[1:2, at]
-        return carry
-
-    lax.fori_loop(0, nrow, lay, 0)
-
-    def owned(values):
-        return (values >= first) & (values < first + ROWS)
-
-    def keys_of(src, tgt):
-        return (src * (NP * ROWS) + tgt + 1).astype(F32)
-
-    def ends(key):
-        code = key.astype(I32) - 1
-        empty = code < 0
-        return (
-            jnp.where(empty, -1, lax.div(code, NP * ROWS)),
-            jnp.where(empty, -1, lax.rem(code, NP * ROWS)),
-        )
-
-    half = ZC * ROWS // 2
-
-    def place(node):
-        part = lax.div(node, ROWS)
-        core = lax.rem(part, C)
-        py = lax.rem(lax.div(part, C), Y)
-        pz = lax.rem(lax.div(part, C * Y), Z)
-        px = lax.div(part, C * Y * Z)
-        inner = (pz * C + core) * ROWS + lax.rem(node, ROWS)
-        spot = lax.div(inner, half) * (XY * half) + (px * Y + py) * half + lax.rem(inner, half)
-        return jnp.where(node < 0, -1, spot)
-
-    near = jnp.where(lane < ROWS, lane + first, -2)
-    near_t = jnp.where(sub < ROWS, sub + first, -2)
-
-    def fill(t_lanes, s_lanes):
-        (t_src, t_tgt), (s_src, s_tgt) = ends(t_lanes), ends(s_lanes)
-        t_far, s_far = place(t_src), place(s_tgt)
-        for g in range(NP * ROWS // TILE):
-            o_top[0:TILE, g * TILE : (g + 1) * TILE] = hot(t_far == lane + g * TILE)
-            o_top[TILE:, g * TILE : (g + 1) * TILE] = hot(s_far == lane + g * TILE)
-        l_top[0:TILE, :] = hot(t_tgt == near)
-        l_top[TILE:, :] = hot(s_src == near)
-        sc_top[0:TILE, :] = hot(ends(jnp.transpose(t_lanes))[1] == near_t)
-        sc_top[TILE:, :] = hot(ends(jnp.transpose(s_lanes))[0] == near_t)
-
-    def fill_row(r):
-        src, tgt = te_s[pl.ds(r, 1), :], te_s[pl.ds(TILE + r, 1), :]
-        key = keys_of(src, tgt)
-        fill(
-            down_lanes(jnp.where(owned(tgt), key, 0.0)), down_lanes(jnp.where(owned(src), key, 0.0))
-        )
-
-    if packed:
-        upper_ones = hot(sub <= lane)
-        lower_ones = hot(lane < sub)
-        sub_f = sub.astype(F32)
-        key_s[...] = keys_of(te_s[0:TILE, :], te_s[TILE:, :])
-        lists = []
-        for values in (te_s[TILE:, :], te_s[0:TILE, :]):
-            mine = owned(values)
-            flags = hot(mine)
-            offset = mm(lower_ones, mm(flags, ones).astype(BF))
-            pos_s[...] = jnp.where(mine, mm(flags, upper_ones) + offset - 1.0, -1.0)
-
-            def pick(r, acc):
-                at = pl.ds(pl.multiple_of(r * 8, 8), 8)
-                places, keys8 = pos_s[at, :], key_s[at, :]
-                for i in range(8):
-                    acc = acc + jnp.where(places[i : i + 1, :] == sub_f, keys8[i : i + 1, :], 0.0)
-                return acc
-
-            acc = lax.fori_loop(0, -(-nrow // 8), pick, jnp.zeros((TILE, TILE), F32))
-            lists.append(jnp.broadcast_to(jnp.sum(acc, axis=1, keepdims=True), (TILE, TILE)))
-        fill(*lists)
-
-    arrived(e0_in)
-    lower = jnp.where(has_dn, e0r[0 : 2 * nc, :], 0.0)
-    grad_coarse0 = lift[:nc] + lower[:nc]
-    den = jnp.maximum(counts[:nc] + lower[nc:], 1.0)
-    den_up = jnp.maximum(e0dr[...] + counts[nc:], 1.0)
-    den_dn = jnp.maximum(e0r[2 * nc :, :] + jnp.where(has_dn2, e0ur[...], 0.0), 1.0)
-    top_g = fold(mm(top_t, pad_rows(wide(grad_coarse0))))
-    e1s[0, 0:ROWS, :] = top_counts[0:ROWS]
-    e1s[0, ROWS:, :] = top_g[0:ROWS]
-    e1s[1, 0:ROWS, :] = top_counts[2 * ROWS : 3 * ROWS]
-    e1s[1, ROWS:, :] = top_g[2 * ROWS : 3 * ROWS]
-    e1_in = [send(e1s.at[0], e1r.at[0], dn_dev), send(e1s.at[1], e1r.at[1], up_dev)]
 
     arrived(halo_in)
     halo_rows = sub
@@ -339,6 +243,9 @@
         return carry
 
     lax.fori_loop(0, ne // step, forward, 0)
+
+    loads["nw"].wait()
+    loads["nb"].wait()
 
     def node_forward(rows, agg, level):
         act = mm(rows, nw_ref[level, :W, :]) + mm(agg, nw_ref[level, W:, :]) + nb_ref[level : level + 1, :]
@@ -370,10 +277,22 @@
     psd[...] = pooled[:rim]
     psu[...] = pooled[2 * nc - rim :]
     ps_in = [send(pss, psr, up_dev), send(psd, psdr, dn_dev), send(psu, psur, up2_dev)]
-    arrived(e1_in)
+    loads["ce"].wait()
+    for k in range(ctile):
+        src = ce_ref[0, 0:1, k * TILE : (k + 1) * TILE]
+        tgt = ce_ref[0, 1:2, k * TILE : (k + 1) * TILE]
+        gcat[k * TILE : (k + 1) * TILE, 0:TILE] = hot(down_lanes(src) == lane)
+        gcat[k * TILE : (k + 1) * TILE, TILE:] = hot(down_lanes(tgt) == lane)
+        gcat_t[0:TILE, k * TILE : (k + 1) * TILE] = hot(sub == src)
+        gcat_t[TILE:, k * TILE : (k + 1) * TILE] = hot(sub == tgt)
+
+    arrived(e0_in)
+    lower_counts = jnp.where(has_dn, e0r[0:nc, :], 0.0)
+    den = jnp.maximum(counts[:nc] + lower_counts, 1.0)
+    den_up = jnp.maximum(e0dr[...] + counts[nc:], 1.0)
+    den_dn = jnp.maximum(e0r[nc:, :] + jnp.where(has_dn2, e0ur[...], 0.0), 1.0)
     own_win = slice(ROWS, 2 * ROWS)
     top_den = jnp.maximum(top_counts[own_win] + e1r[0, 0:ROWS, :] + e1r[1, 0:ROWS, :], 1.0)
-    top_grad = pad_rows(top_g[own_win] + e1r[0, ROWS:, :] + e1r[1, ROWS:, :])
     arrived(ps_in)
     start_f = ((pooled[:nc] + jnp.where(has_dn, psr[rim:, :], 0.0)) / den).astype(BF).astype(F32)
     left = (psr[0:rim, :] + jnp.where(has_dn2, psur[...], 0.0)) / den_dn
@@ -397,6 +316,86 @@
     tss[0] = top_part[0:ROWS]
     tss[1] = top_part[2 * ROWS : 3 * ROWS]
     ts_in = [send(tss.at[0], tsr.at[0], dn_dev), send(tss.at[1], tsr.at[1], up_dev)]
+    first = p * ROWS
+
+    def owned(values):
+        return (values >= first) & (values < first + ROWS)
+
+    def keys_of(src, tgt):
+        return (src * (NP * ROWS) + tgt + 1).astype(F32)
+
+    def ends(key):
+        code = key.astype(I32) - 1
+        empty = code < 0
+        return (
+            jnp.where(empty, -1, lax.div(code, NP * ROWS)),
+            jnp.where(empty, -1, lax.rem(code, NP * ROWS)),
+        )
+
+    def place(node):
+        part = lax.div(node, ROWS)
+        core = lax.rem(part, C)
+        py = lax.rem(lax.div(part, C), Y)
+        pz = lax.rem(lax.div(part, C * Y), Z)
+        px = lax.div(part, C * Y * Z)
+        inner = (pz * C + core) * ROWS + lax.rem(node, ROWS)
+        spot = lax.div(inner, half) * (XY * half) + (px * Y + py) * half + lax.rem(inner, half)
+        return jnp.where(node < 0, -1, spot)
+
+    half = ZC * ROWS // 2
+    near = jnp.where(lane < ROWS, lane + first, -2)
+    near_t = jnp.where(sub < ROWS, sub + first, -2)
+
+    def fill(t_lanes, s_lanes):
+        (t_src, t_tgt), (s_src, s_tgt) = ends(t_lanes), ends(s_lanes)
+        t_far, s_far = place(t_src), place(s_tgt)
+        for g in range(NP * ROWS // TILE):
+            o_top[0:TILE, g * TILE : (g + 1) * TILE] = hot(t_far == lane + g * TILE)
+            o_top[TILE:, g * TILE : (g + 1) * TILE] = hot(s_far == lane + g * TILE)
+        l_top[0:TILE, :] = hot(t_tgt == near)
+        l_top[TILE:, :] = hot(s_src == near)
+        sc_top[0:TILE, :] = hot(ends(jnp.transpose(t_lanes))[1] == near_t)
+        sc_top[TILE:, :] = hot(ends(jnp.transpose(s_lanes))[0] == near_t)
+
+    def fill_row(r):
+        src, tgt = te_s[pl.ds(r, 1), :], te_s[pl.ds(TILE + r, 1), :]
+        key = keys_of(src, tgt)
+        fill(
+            down_lanes(jnp.where(owned(tgt), key, 0.0)), down_lanes(jnp.where(owned(src), key, 0.0))
+        )
+
+    loads["te"].wait()
+    te_s[...] = jnp.full(te_s.shape, -1, I32)
+
+    def lay(r, carry):
+        at = pl.ds(pl.multiple_of(r * TILE, TILE), TILE)
+        te_s[pl.ds(r, 1), :] = te_ref[0:1, at]
+        te_s[pl.ds(TILE + r, 1), :] = te_ref[1:2, at]
+        return carry
+
+    lax.fori_loop(0, nrow, lay, 0)
+
+    if packed:
+        upper_ones = hot(sub <= lane)
+        lower_ones = hot(lane < sub)
+        sub_f = sub.astype(F32)
+        key_s[...] = keys_of(te_s[0:TILE, :], te_s[TILE:, :])
+        lists = []
+        for values in (te_s[TILE:, :], te_s[0:TILE, :]):
+            mine = owned(values)
+            flags = hot(mine)
+            offset = mm(lower_ones, mm(flags, ones).astype(BF))
+            pos_s[...] = jnp.where(mine, mm(flags, upper_ones) + offset - 1.0, -1.0)
+
+            def pick(r, acc):
+                at = pl.ds(pl.multiple_of(r * 8, 8), 8)
+                places, keys8 = pos_s[at, :], key_s[at, :]
+                for i in range(8):
+                    acc = acc + jnp.where(places[i : i + 1, :] == sub_f, keys8[i : i + 1, :], 0.0)
+                return acc
+
+            acc = lax.fori_loop(0, -(-nrow // 8), pick, jnp.zeros((TILE, TILE), F32))
+            lists.append(jnp.broadcast_to(jnp.sum(acc, axis=1, keepdims=True), (TILE, TILE)))
     arrived(ts_in)
     top_start = ((top_part[own_win] + tsr[0] + tsr[1]) / top_den).astype(BF)
 
@@ -413,7 +412,33 @@
         yield
         arrived(copies)
 
-    for _ in gather(top_start.astype(F32), cb1, tab1):
+    first_gather = gather(top_start.astype(F32), cb1, tab1)
+    next(first_gather)
+    if packed:
+        fill(*lists)
+
+    next(first_gather)
+
+    loads["cot"].wait()
+    gout = cot_ref[...] * alive
+    lift = fold(mm(pool_t[...], wide(gout)))
+    lfs[...] = lift[nc:]
+    lf_in = [send(lfs, lfr, up_dev)]
+    top_l = hot(down_lanes(rel) == lane)
+    for g in range(nf // TILE):
+        keys = pm_ref[0:1, g * TILE : (g + 1) * TILE]
+        pool_l[g * TILE : (g + 1) * TILE, :] = hot((down_lanes(keys) == lane) & (sub + g * TILE < live))
+    next(first_gather)
+    arrived(lf_in)
+    grad_coarse0 = lift[:nc] + jnp.where(has_dn, lfr[...], 0.0)
+    top_g = fold(mm(top_t, pad_rows(wide(grad_coarse0))))
+    e1s[0, ROWS:, :] = top_g[0:ROWS]
+    e1s[1, ROWS:, :] = top_g[2 * ROWS : 3 * ROWS]
+    e1_in = [
+        send(e1s.at[0, ROWS:], e1r.at[0, ROWS:], dn_dev),
+        send(e1s.at[1, ROWS:], e1r.at[1, ROWS:], up_dev),
+    ]
+    for _ in first_gather:
         pass
 
     ws2, wt2, mb2 = mw_ref[2, :W, :], mw_ref[2, W:, :], mb_ref[2:3, :]
@@ -484,6 +509,8 @@
         over_rows(lambda: (t_sums(t_edges()[2]),))
         agg_t = sums_r[0].astype(BF)
     t_hidden, act_slope_t = node_forward(top_rows, agg_t, 2)
+    arrived(e1_in)
+    top_grad = pad_rows(top_g[own_win] + e1r[0, ROWS:, :] + e1r[1, ROWS:, :])
     g_nodes, g_agg, dwn2_a, dwn2_b, dbn2 = node_backward(top_rows, agg_t, act_slope_t, top_grad, 2)
     kept[:, W:] = g_agg
     key_s[...] = g_nodes
@@ -601,7 +628,6 @@
         rgr[0:nc, :] + jnp.concatenate([rus[...], middle, jnp.where(has_up2, rdr[...], 0.0)], axis=0)
     ) / den_up
     pool_grad = jnp.concatenate([g_csum, jnp.where(has_up, upper, 0.0)], axis=0)
-    next(reduce_a)
     grad_fine = gout + fold(mm(pool_l[...], wide(pool_grad)))
 
     g_nodes, g_agg, dwn0_a, dwn0_b, dbn0 = node_backward(x_ref[...], aggf[...], act_slope[...], grad_fine, 0)
@@ -730,7 +756,7 @@
         vm(nf, W), vb(nf, W), vb(nf, W), vb(TILE, nf), vb(nf, TILE),
         vb(nec, 2 * TILE), vb(2 * TILE, nec), vb(2 * TILE, NP * ROWS), vb(2 * TILE, TILE),
         vb(2 * TILE, TILE), pltpu.VMEM((2 * TILE, TILE), I32), vm(TILE, TILE), vm(TILE, TILE),
-        vb(128, W), vb(128, W), vm(2 * nc + 8, W), vm(2 * nc + 8, W), vm(nc, W), vm(nc, W),
+        vb(128, W), vb(128, W), vm(nc, W), vm(nc, W), vm(nc + 8, W), vm(nc + 8, W), vm(nc, W), vm(nc, W),
         vm(8, W), vm(8, W), vm(2, 16, W), vm(2, 16, W),
         vm(nc + 8, W), vm(nc + 8, W), vm(8, W), vm(8, W), vm(8, W), vm(8, W),
         vm(2, 8, W), vm(2, 8, W),
@@ -739,7 +765,7 @@
         vm(nc + 8, W), vm(nc + 8, W), vm(8, W), vm(8, W), vm(8, W), vb(128, W), vb(128, W),
         *reduce_bufs(4 * W), *reduce_bufs(8 * W),
     ]
-    copies = 24 + 2 * (X * Y + Z * C) + 2 * (2 * X * Y + Z)
+    copies = 28 + 2 * (X * Y + Z * C) + 2 * (2 * X * Y + Z)
     scratch += [pltpu.SemaphoreType.DMA((copies,)), pltpu.SemaphoreType.DMA((copies,))]
     in_hbm = pl.BlockSpec(memory_space=pltpu.HBM)
     sizes = (X, Z, Y, C, nf, ne, nc, nec, et // TILE)
@@ -756,14 +782,30 @@
     )(*args)
 
 
+def lists_kernel(te_in, fit_ref, te, sem):
+    load = pltpu.make_async_copy(te_in, te, sem)
+    load.start()
+    load.wait()
+    most = 0.0
+    for end in range(2):
+        owner = lax.div(te[end : end + 1, :], ROWS)
+        digits = iota((16, te.shape[1]), 0)
+        counts = nt(hot(lax.div(owner, 16) == digits), hot(lax.rem(owner, 16) == digits))
+        most = jnp.maximum(most, jnp.max(counts))
+    fit_ref[0] = (most <= CAP).astype(I32)
+
+
 def per_device(split, *args):
-    owner = args[-1] // ROWS
-    digits = jnp.arange(16)[None, :, None]
-    high = (owner[:, None, :] // 16 == digits).astype(BF)
-    low = (owner[:, None, :] % 16 == digits).astype(BF)
-    counts = jnp.einsum("khe,kle->khl", high, low, preferred_element_type=F32)
+    fit = pl.pallas_call(
+        lists_kernel,
+        out_shape=jax.ShapeDtypeStruct((1,), I32),
+        in_specs=[pl.BlockSpec(memory_space=pltpu.HBM)],
+        out_specs=pl.BlockSpec(memory_space=pltpu.SMEM),
+        scratch_shapes=[pltpu.VMEM(args[-1].shape, I32), pltpu.SemaphoreType.DMA],
+        name="lists",
+    )(args[-1])
     outs = lax.cond(
-        jnp.max(counts) <= CAP,
+        fit[0] > 0,
         functools.partial(one_step, split, True),
         functools.partial(one_step, split, False),
         *args,

time: 109 us -> 105 us (0.963)
  other arithmetic: 1.48 us -> 0 us
  matrix products: 1.15 us -> 0 us
    pallas_call x1, Pallas kernels: 102 us -> 98.7 us  [one_step(): pl.pallas_call(functools.partial(step_kernel, sizes, packed), out_shape=o...]
    pallas_call x0 -> x1, Pallas kernels: none -> 2.07 us  [per_device(): pl.pallas_call(lists_kernel, out_shape=jax.ShapeDtypeStruct((1,), I32), i...]
    select_n x2 -> x0, other arithmetic: 1.48 us -> none  [the longest x1 1.33 us: per_device(): high = (owner[:, None, :] // 16 == digits).astype(BF)]
    dot_general x1 -> x0, matrix products: 1.15 us -> none  [per_device(): counts = jnp.einsum('khe,kle->khl', high, low, preferred_element_type=F32)]
where the time goes in v1:
time: 105 us
  Pallas kernels  103 us (98%)
  between operations  1.46 us (1%)
    pallas_call x1, Pallas kernels, one_step(): pl.pallas_call(functools.partial(step_kernel, sizes, packed), out_shape=o...  98.7 us
    pallas_call x1, Pallas kernels, per_device(): pl.pallas_call(parts_kernel, out_shape=[jax.ShapeDtypeStruct(a.shape, t)...  2.16 us

profile of v1, /device:TPU:1, one launch (start us, length us, event | category | flops | bytes accessed | tf_op | source)
XLA Modules:
  0.0 104.5 jit_solution(17594942252962803714)
XLA Ops:
  0.6 2.1 %lists.1 = s32[1]{0:T(128)} custom-call(s32[2,12288]{1,0:T(2,128)} %te_in.1), custom_call_target="tpu_custom_call" | custom-call | tf_op jit(solution)/shard_map/lists/pallas_call | solution.py:799
  3.4 98.9 %conditional.1 = ((bf16[512,128]{1,0:T(8,128)(2,1)}, f32[512,128]{1,0:T(8,128)}, f32[1552,128]{1,0:T(8,128)})) conditional(s32[]{:T(128)} %bitcast, (bf16[512,128]{1,0:T(8,128)(2,1)}, f32[512,128]{1,0:T(8,128)}, bf16[3,256,128]{2,1,0:T(8,128)(2,1)}, f32[3,128]{1,0:T(4,128)}, bf16[3,256,128]{2,1,0:T(8,128)(2,1)}, /*index=5*/f32[3,128]{1,0:T(4,128)}, ...), branch_computations={%region_0.0_spmd, %region_1.0_spmd} | conditional | bytes 8 | solution.py:807
  3.6 98.7 %step.1 = (bf16[512,128]{1,0:T(8,128)(2,1)}, f32[512,128]{1,0:T(8,128)}, f32[1552,128]{1,0:T(8,128)}) custom-call(bf16[512,128]{1,0:T(8,128)(2,1)} %get-tuple-element.65.x_in, f32[512,128]{1,0:T(8,128)} %get-tuple-element.66.cot_in, bf16[3,256,128]{2,1,0:T(8,128)(2,1)} %get-tuple-element.67.mw_in, f32[3,128]{1,0:T(4,128)} %get-tuple-element.68.mb_in, ...), custom_call_target="tpu_custom_call" | custom-call | tf_op jit(solution)/shard_map/cond/branch_1_fun/step/pallas_call | solution.py:772
  102.2 2.2 %parts.1 = (bf16[512,128]{1,0:T(8,128)(2,1)}, f32[512,128]{1,0:T(8,128)}, f32[3,256,128]{2,1,0:T(8,128)}, f32[3,128]{1,0:T(4,128)}, f32[3,256,128]{2,1,0:T(8,128)}, /*index=5*/f32[3,128]{1,0:T(4,128)}) custom-call(bf16[512,128]{1,0:T(8,128)(2,1)} %get-tuple-element.87.out_in, f32[512,128]{1,0:T(8,128)} %get-tuple-element.88.grad_in, ...), custom_call_target="tpu_custom_call" | custom-call | tf_op jit(solution)/shard_map/parts/pallas_call | solution.py:817
